TPU v7x, 32 devices: a whole 2x2x4 slice. The times are simulated.
32 devices in a mesh: dp: 4 (over z), ctx: 8 (over y, x, core).
Axes of the slice: x: 2, y: 2, z: 4, core: 2. Of those that a mesh axis runs over, the one named last changes fastest.
Arguments:
- hidden_in: bfloat16 [4, 1024, 768], P('dp', 'ctx'), may hold values from -6 to 6
- segment_ids: int32 [4, 1024], P('dp', 'ctx'), may hold values from 0 to 4, as said below
- w_qkv: bfloat16 [768, 2304], P('dp'), may hold values from -0.21875 to 0.21875
- w_out: bfloat16 [768, 768], P('dp'), may hold values from -4 to 4
- w_in: bfloat16 [768, 2304], P('dp'), may hold values from -0.21875 to 0.21875
- w_down: bfloat16 [1152, 768], P('dp'), may hold values from -0.1875 to 0.1875
- gain_attn: bfloat16 [768], P('dp'), may hold values from 0.5 to 1.5
- gain_mlp: bfloat16 [768], P('dp'), may hold values from 0.5 to 1.5
- cotangent: bfloat16 [4, 1024, 768], P('dp', 'ctx'), may hold values from -6 to 6
Outputs:
- output: bfloat16 [4, 1024, 768], P('dp', 'ctx')
- grad_input: float32 [4, 1024, 768], P('dp', 'ctx')
- grad_qkv: float32 [768, 2304], P('dp')
- grad_out: float32 [768, 768], P('dp')
- grad_in: float32 [768, 2304], P('dp')
- grad_down: float32 [1152, 768], P('dp')
- grad_gain_attn: float32 [768], P('dp')
- grad_gain_mlp: float32 [768], P('dp')
Inputs may be any that keep to these rules, and one draw needn't show every extreme that they name: `segment_ids`: ids never fall along a sequence; each sequence holds documents 0 to 4; document 2 begins within the first 128 tokens and ends within the last 128; every other document is shorter than 128 tokens.
All inputs are finite; a program needn't handle non-finite values.
Results may differ from a plain program's by a relative error of at most 0.024.
Values may be sent and summed in bfloat16 or wider, within the bound.
A program may use at most 256 MiB of HBM per device.

v0:
```python
import jax
import jax.numpy as jnp
from jax import lax
from jax.sharding import PartitionSpec as P

HEADS = 12
EPSILON = 1e-05
ROPE_THETA = 160000.0
NEGATIVE = -1e30


def layer_norm(values, gain_row):
    average = jnp.mean(values, axis=-1, keepdims=True)
    centred = values - average
    spread = jnp.mean(centred * centred, axis=-1, keepdims=True)
    return centred * lax.rsqrt(spread + EPSILON) * gain_row


def rope_tables(first_row, row_count, head_size):
    position = (first_row + jnp.arange(row_count, dtype=jnp.int32)).astype(jnp.float32)
    frequency = ROPE_THETA ** (-jnp.arange(0, head_size, 2, dtype=jnp.float32) / head_size)
    angles = position[:, None] * frequency[None, :]
    angles = jnp.concatenate([angles, angles], axis=-1)
    return (jnp.cos(angles)[:, None, :], jnp.sin(angles)[:, None, :])


def rotary(values, cosines, sines):
    half_size = values.shape[-1] // 2
    turned = jnp.concatenate([-values[..., half_size:], values[..., :half_size]], axis=-1)
    return values * cosines + turned * sines


def rotary_back(grads, cosines, sines):
    half_size = grads.shape[-1] // 2
    shifted = grads * sines
    return grads * cosines + jnp.concatenate(
        [shifted[..., half_size:], -shifted[..., :half_size]], axis=-1
    )


def geglu(gate_in, gate_up):
    return jax.nn.gelu(gate_in, approximate=False) * gate_up


def contract_rows(left_side, right_side):
    return lax.dot_general(
        left_side, right_side, (((0,), (0,)), ((), ())), preferred_element_type=jnp.float32
    )


def contract_cols(left_side, right_side):
    return lax.dot_general(
        left_side, right_side, (((1,), (1,)), ((), ())), preferred_element_type=jnp.float32
    )


def local(hidden_in, segment_ids, w_qkv, w_out, w_in, w_down, gain_attn, gain_mlp, cotangent):
    local_rows = hidden_in.shape[1]
    model_width = hidden_in.shape[2]
    head_count = HEADS
    head_size = model_width // head_count
    score_scale = head_size ** (-0.5)
    head_shape = (local_rows, head_count, head_size)
    shards = (w_qkv, w_out, w_in, w_down, gain_attn, gain_mlp)
    qkv_full, out_full, in_full, down_full, attn_scale, mlp_scale = (
        lax.all_gather(shards[0], "dp", axis=0, tiled=True),
        lax.all_gather(shards[1], "dp", axis=0, tiled=True),
        lax.all_gather(shards[2], "dp", axis=0, tiled=True),
        lax.all_gather(shards[3], "dp", axis=0, tiled=True),
        lax.all_gather(shards[4], "dp", axis=0, tiled=True),
        lax.all_gather(shards[5], "dp", axis=0, tiled=True),
    )
    hidden_units = in_full.shape[1] // 2
    source = hidden_in[0].astype(jnp.float32)
    own_ids = segment_ids[0]
    cosines, sines = rope_tables(lax.axis_index("ctx") * local_rows, local_rows, head_size)
    normed_one = layer_norm(source, attn_scale.astype(jnp.float32)).astype(jnp.bfloat16)
    projected = jnp.dot(normed_one, qkv_full, preferred_element_type=jnp.float32)
    queries = rotary(projected[:, :model_width].reshape(head_shape), cosines, sines).astype(
        jnp.bfloat16
    )
    own_keys = rotary(
        projected[:, model_width : 2 * model_width].reshape(head_shape), cosines, sines
    ).astype(jnp.bfloat16)
    value_flat = projected[:, 2 * model_width :].astype(jnp.bfloat16)
    own_values = value_flat.reshape(head_shape)
    key_flat = own_keys.reshape(local_rows, model_width)
    query_flat = queries.reshape(local_rows, model_width)
    highest = jnp.full((head_count, local_rows), NEGATIVE, jnp.float32)
    block_keys = lax.all_gather(key_flat, "ctx", axis=0, tiled=True)
    block_values = lax.all_gather(value_flat, "ctx", axis=0, tiled=True)
    block_ids = lax.all_gather(own_ids, "ctx", axis=0, tiled=True)
    piece_rows = block_keys.shape[0]
    scores = (
        jnp.einsum(
            "qhe,khe->hqk",
            queries,
            block_keys.reshape(piece_rows, head_count, head_size),
            preferred_element_type=jnp.float32,
        )
        * score_scale
    )
    allowed = (own_ids[:, None] == block_ids[None, :])[None]
    scores = jnp.where(allowed, scores, NEGATIVE)
    raised = jnp.maximum(highest, jnp.max(scores, axis=-1))
    weights = jnp.where(allowed, jnp.exp(scores - raised[..., None]), 0.0)
    row_total = jnp.sum(weights, axis=-1)
    update = jnp.einsum(
        "hqk,khe->qhe",
        weights.astype(jnp.bfloat16),
        block_values.reshape(piece_rows, head_count, head_size),
        preferred_element_type=jnp.float32,
    )
    summed = update
    highest, row_total, summed = (raised, row_total, summed)
    attention = summed / jnp.transpose(row_total)[:, :, None]
    log_total = highest + jnp.log(row_total)
    attended = attention.reshape(local_rows, model_width).astype(jnp.bfloat16)
    middle = source + jnp.dot(attended, out_full, preferred_element_type=jnp.float32)
    normed_two = layer_norm(middle, mlp_scale.astype(jnp.float32)).astype(jnp.bfloat16)
    lifted = jnp.dot(normed_two, in_full, preferred_element_type=jnp.float32)
    gate_in = lifted[:, :hidden_units]
    gate_up = lifted[:, hidden_units:]
    mixed_units = geglu(gate_in, gate_up).astype(jnp.bfloat16)
    result = (middle + jnp.dot(mixed_units, down_full, preferred_element_type=jnp.float32)).astype(
        jnp.bfloat16
    )
    qkv_back, out_back, in_back, down_back, attn_back, mlp_back = (
        lax.all_gather(shards[0], "dp", axis=0, tiled=True),
        lax.all_gather(shards[1], "dp", axis=0, tiled=True),
        lax.all_gather(shards[2], "dp", axis=0, tiled=True),
        lax.all_gather(shards[3], "dp", axis=0, tiled=True),
        lax.all_gather(shards[4], "dp", axis=0, tiled=True),
        lax.all_gather(shards[5], "dp", axis=0, tiled=True),
    )
    upstream = cotangent[0]
    grad_down = contract_rows(mixed_units, upstream)
    grad_mixed = contract_cols(upstream, down_back)
    _, pull_gate = jax.vjp(geglu, gate_in, gate_up)
    grad_gate_in, grad_gate_up = pull_gate(grad_mixed)
    grad_lifted = jnp.concatenate([grad_gate_in, grad_gate_up], axis=1).astype(jnp.bfloat16)
    grad_in = contract_rows(normed_two, grad_lifted)
    grad_normed_two = contract_cols(grad_lifted, in_back)
    _, pull_two = jax.vjp(layer_norm, middle, mlp_back.astype(jnp.float32))
    grad_middle_part, grad_mlp_gain = pull_two(grad_normed_two)
    grad_middle = upstream.astype(jnp.float32) + grad_middle_part
    grad_branch = grad_middle.astype(jnp.bfloat16)
    grad_out = contract_rows(attended, grad_branch)
    grad_attended = contract_cols(grad_branch, out_back).astype(jnp.bfloat16)
    grad_heads = grad_attended.reshape(head_shape)
    products = jnp.transpose(jnp.sum(grad_heads.astype(jnp.float32) * attention, axis=-1))
    all_log, all_products, all_ids = (
        lax.all_gather(log_total, "ctx", axis=1, tiled=True),
        lax.all_gather(products, "ctx", axis=1, tiled=True),
        lax.all_gather(own_ids, "ctx", axis=0, tiled=True),
    )
    block_keys = lax.all_gather(key_flat, "ctx", axis=0, tiled=True)
    block_values = lax.all_gather(value_flat, "ctx", axis=0, tiled=True)
    block_ids = lax.all_gather(own_ids, "ctx", axis=0, tiled=True)
    piece_rows = block_keys.shape[0]
    key_heads = block_keys.reshape(piece_rows, head_count, head_size)
    scores = (
        jnp.einsum("qhe,khe->hqk", queries, key_heads, preferred_element_type=jnp.float32)
        * score_scale
    )
    allowed = (own_ids[:, None] == block_ids[None, :])[None]
    probabilities = jnp.where(allowed, jnp.exp(scores - log_total[..., None]), 0.0)
    grad_probs = jnp.einsum(
        "qhe,khe->hqk",
        grad_heads,
        block_values.reshape(piece_rows, head_count, head_size),
        preferred_element_type=jnp.float32,
    )
    grad_scores = (probabilities * (grad_probs - products[..., None])).astype(jnp.bfloat16)
    grad_queries = score_scale * jnp.einsum(
        "hqk,khe->qhe", grad_scores, key_heads, preferred_element_type=jnp.float32
    )
    block_queries = lax.all_gather(query_flat, "ctx", axis=0, tiled=True)
    block_grads = lax.all_gather(grad_attended, "ctx", axis=0, tiled=True)
    piece_rows = block_queries.shape[0]
    query_heads = block_queries.reshape(piece_rows, head_count, head_size)
    grad_rows = block_grads.reshape(piece_rows, head_count, head_size)
    scores = (
        jnp.einsum("qhe,khe->hqk", query_heads, own_keys, preferred_element_type=jnp.float32)
        * score_scale
    )
    allowed = (all_ids[:, None] == own_ids[None, :])[None]
    probabilities = jnp.where(allowed, jnp.exp(scores - all_log[..., None]), 0.0)
    grad_values = jnp.einsum(
        "hqk,qhe->khe",
        probabilities.astype(jnp.bfloat16),
        grad_rows,
        preferred_element_type=jnp.float32,
    )
    grad_probs = jnp.einsum(
        "qhe,khe->hqk", grad_rows, own_values, preferred_element_type=jnp.float32
    )
    grad_scores = (probabilities * (grad_probs - all_products[..., None])).astype(jnp.bfloat16)
    grad_keys = score_scale * jnp.einsum(
        "hqk,qhe->khe", grad_scores, query_heads, preferred_element_type=jnp.float32
    )
    grad_keys, grad_values = (grad_keys, grad_values)
    grad_projected = jnp.concatenate(
        [
            rotary_back(grad_queries, cosines, sines).reshape(local_rows, model_width),
            rotary_back(grad_keys, cosines, sines).reshape(local_rows, model_width),
            grad_values.reshape(local_rows, model_width),
        ],
        axis=1,
    ).astype(jnp.bfloat16)
    grad_qkv = contract_rows(normed_one, grad_projected)
    grad_normed_one = contract_cols(grad_projected, qkv_back)
    _, pull_one = jax.vjp(layer_norm, source, attn_back.astype(jnp.float32))
    grad_source, grad_attn_gain = pull_one(grad_normed_one)
    grad_input = grad_middle + grad_source
    local_grads = (grad_qkv, grad_out, grad_in, grad_down, grad_attn_gain, grad_mlp_gain)
    shares = (
        lax.psum_scatter(
            local_grads[0].astype(jnp.bfloat16), "dp", scatter_dimension=0, tiled=True
        ).astype(jnp.float32),
        lax.psum_scatter(
            local_grads[1].astype(jnp.bfloat16), "dp", scatter_dimension=0, tiled=True
        ).astype(jnp.float32),
        lax.psum_scatter(
            local_grads[2].astype(jnp.bfloat16), "dp", scatter_dimension=0, tiled=True
        ).astype(jnp.float32),
        lax.psum_scatter(
            local_grads[3].astype(jnp.bfloat16), "dp", scatter_dimension=0, tiled=True
        ).astype(jnp.float32),
        lax.psum_scatter(
            local_grads[4].astype(jnp.bfloat16), "dp", scatter_dimension=0, tiled=True
        ).astype(jnp.float32),
        lax.psum_scatter(
            local_grads[5].astype(jnp.bfloat16), "dp", scatter_dimension=0, tiled=True
        ).astype(jnp.float32),
    )
    shares = (
        lax.psum(shares[0].astype(jnp.bfloat16), "ctx").astype(jnp.float32),
        lax.psum(shares[1].astype(jnp.bfloat16), "ctx").astype(jnp.float32),
        lax.psum(shares[2].astype(jnp.bfloat16), "ctx").astype(jnp.float32),
        lax.psum(shares[3].astype(jnp.bfloat16), "ctx").astype(jnp.float32),
        lax.psum(shares[4].astype(jnp.bfloat16), "ctx").astype(jnp.float32),
        lax.psum(shares[5].astype(jnp.bfloat16), "ctx").astype(jnp.float32),
    )
    return (
        result[None],
        grad_input[None],
        shares[0],
        shares[1],
        shares[2],
        shares[3],
        shares[4],
        shares[5],
    )


def solution(mesh):
    in_specs = (
        P("dp", "ctx", None),
        P("dp", "ctx"),
        P("dp", None),
        P("dp", None),
        P("dp", None),
        P("dp", None),
        P("dp"),
        P("dp"),
        P("dp", "ctx", None),
    )
    out_specs = (
        P("dp", "ctx", None),
        P("dp", "ctx", None),
        P("dp", None),
        P("dp", None),
        P("dp", None),
        P("dp", None),
        P("dp"),
        P("dp"),
    )
    return jax.shard_map(local, mesh=mesh, in_specs=in_specs, out_specs=out_specs, check_vma=False)
```

profile of v0, /device:TPU:0, one launch (start us, length us, event | category | flops | bytes accessed | tf_op | source)
XLA Modules:
  0.0 630.1 jit_solution(16062213591360769307)
XLA Ops:
  8.0 1.3 fusion.87
  11.6 13.6 %all-reduce.7 = (bf16[768]{0:T(1024)(128)(2,1)S(1)}, bf16[768]{0:T(1024)(128)(2,1)S(1)}) all-reduce(bf16[768]{0:T(1024)(128)(2,1)S(1)} %dynamic-update-slice, bf16[768]{0:T(1024)(128)(2,1)S(1)} %dynamic-update-slice.1), channel_id=1, replica_groups=mesh['dp'=4,'ctx'=8] {'dp'}, use_global_device_ids=true, to_apply=%add | all-reduce | flops 1536 | bytes 6144
  28.5 53.9 %all-gather.10.cloned.1.call-done = bf16[768,2304]{1,0:T(8,128)(2,1)} async-done(((bf16[192,2304]{1,0:T(8,128)(2,1)}), bf16[768,2304]{1,0:T(8,128)(2,1)}) %all-gather.10.cloned.1.call-update) | async-done | bytes 3538960 | tf_op jit(solution)/shard_map/all_gather | solution.py:66
  82.3 2.8 fusion.78
  87.6 2.0 add_convert_fusion.2
  92.2 8.7 %all-gather = s32[1,1024]{1,0:T(1,128)S(1)} all-gather(s32[1,128]{1,0:T(1,128)S(1)} %copy-done.44), channel_id=2, replica_groups=mesh['dp'=4,'ctx'=8] {'ctx'}, dimensions={1}, use_global_device_ids=true | all-gather | bytes 4608 | tf_op jit(solution)/shard_map/all_gather | solution.py:92
  101.1 12.9 %all-gather.14.cloned.1.call-done = bf16[1024,768]{1,0:T(8,128)(2,1)} async-done(((bf16[128,768]{1,0:T(8,128)(2,1)}), bf16[1024,768]{1,0:T(8,128)(2,1)}) %all-gather.14.cloned.1.call-update) | async-done | bytes 1572880 | tf_op jit(solution)/shard_map/all_gather | solution.py:90
  114.0 1.7 copy.50
  115.7 1.3 select_reduce_fusion
  117.1 2.7 copy-done
  119.7 2.0 fusion.1
  121.7 19.9 %all-gather.12.cloned.1.call-done = bf16[1024,768]{1,0:T(8,128)(2,1)} async-done(((bf16[128,768]{1,0:T(8,128)(2,1)}), bf16[1024,768]{1,0:T(8,128)(2,1)}) %all-gather.12.cloned.1.call-update) | async-done | bytes 1572880 | tf_op jit(solution)/shard_map/all_gather | solution.py:91
  141.6 2.6 copy.45
  144.2 5.8 fusion.88
  150.0 23.5 %all-gather.16.cloned.1.call-done = bf16[768,768]{1,0:T(8,128)(2,1)} async-done(((bf16[192,768]{1,0:T(8,128)(2,1)}), bf16[768,768]{1,0:T(8,128)(2,1)}) %all-gather.16.cloned.1.call-update) | async-done | bytes 1179664 | tf_op jit(solution)/shard_map/all_gather | solution.py:67
  173.5 1.7 fusion.89
  176.0 68.1 %all-gather.18.cloned.1.call-done = bf16[768,2304]{1,0:T(8,128)(2,1)} async-done(((bf16[192,2304]{1,0:T(8,128)(2,1)}), bf16[768,2304]{1,0:T(8,128)(2,1)}) %all-gather.18.cloned.1.call-update) | async-done | bytes 3538960 | tf_op jit(solution)/shard_map/all_gather | solution.py:68
  244.1 2.7 fusion.81
  246.8 37.7 %all-gather.20.cloned.1.call-done = bf16[1152,768]{1,0:T(8,128)(2,1)} async-done(((bf16[288,768]{1,0:T(8,128)(2,1)}), bf16[1152,768]{1,0:T(8,128)(2,1)}) %all-gather.20.cloned.1.call-update) | async-done | bytes 1769488 | tf_op jit(solution)/shard_map/all_gather | solution.py:69
  284.5 3.3 add_convert_fusion
  288.7 1.9 multiply_reduce_fusion
  291.0 1.2 convolution_convert_fusion.4
  292.5 2.4 convolution_convert_fusion.3
  295.0 1.9 convolution_convert_fusion.2
  297.0 3.9 convolution_convert_fusion
  301.0 1.6 broadcast_compare_fusion
  304.5 7.0 %all-gather.22.cloned.1.call-done = bf16[1024,768]{1,0:T(8,128)(2,1)} async-done(((bf16[128,768]{1,0:T(8,128)(2,1)}), bf16[1024,768]{1,0:T(8,128)(2,1)}) %all-gather.22.cloned.1.call-update) | async-done | bytes 1572880 | tf_op jit(solution)/shard_map/all_gather | solution.py:178
  311.5 2.6 copy.54
  314.8 10.1 %all_gather.59 = f32[12,1024]{1,0:T(8,128)} all-gather(f32[12,128]{1,0:T(8,128)S(1)} %log_add_fusion), channel_id=1, replica_groups=mesh['dp'=4,'ctx'=8] {'ctx'}, dimensions={1}, use_global_device_ids=true | all-gather | bytes 55296 | tf_op jit(solution)/shard_map/all_gather | solution.py:153
  326.0 9.1 %all_gather.61 = f32[12,1024]{1,0:T(8,128)} all-gather(f32[12,128]{1,0:T(8,128)S(1)} %bitcast.131), channel_id=1, replica_groups=mesh['dp'=4,'ctx'=8] {'ctx'}, dimensions={1}, use_global_device_ids=true | all-gather | bytes 55296 | tf_op jit(solution)/shard_map/all_gather | solution.py:154
  335.0 5.2 fusion.54
  340.3 2.7 copy.55
  343.0 9.0 %fusion.17 = f32[128,12,64]{0,2,1:T(8,128)} fusion(bf16[1024,12,64]{0,2,1:T(8,128)(2,1)} %bitcast.105, f32[12,1024,128]{2,1,0:T(8,128)} %fusion.54, f32[12,1024]{1,0:T(8,128)S(1)} %copy-done.30, f32[12,1024]{1,0:T(8,128)S(1)} %copy-done.28, pred[1024,128]{1,0:T(8,128)(4,1)S(1)} %copy-done.26, bf16[1024,12,64]{0,2,1:T(8,128)(2,1)} %bitcast.114, ...), kind=kOutput, calls=%fused_computation.22 | convolution fusion | flops 412090368 | bytes 10256384 | tf_op jit(solution)/shard_map/hqk,qhe->khe/dot_general | solution.py:199
  352.0 7.1 %broadcast_multiply_fusion.1 = (f32[128,12,64]{0,2,1:T(8,128)}, f32[128,12,64]{0,2,1:T(8,128)S(1)}, f32[128,12,64]{0,2,1:T(8,128)}) fusion(f32[128,64]{0,1:T(8,128)} %get-tuple-element.47, f32[128,12,64]{0,2,1:T(8,128)} %fusion.17, bf16[1024,12,64]{0,2,1:T(8,128)(2,1)S(1)} %bitcast.103, f32[12,128,1024]{2,1,0:T(8,128)} %copy-done, ...), kind=kOutput, calls=%fused_computation.102 | convolution fusion | flops 412286976 | bytes 11382784 | tf_op jit(solution)/shard_map/hqk,khe->qhe/dot_general | solution.py:175
  359.1 1.2 fusion.85
  360.3 1.3 fusion.48
  361.6 5.0 fusion.23
  367.3 3.0 convolution_convert_fusion.1
  371.4 39.2 %reduce-scatter.11.cloned.1.call-done = bf16[288,768]{1,0:T(8,128)(2,1)} async-done(((bf16[1152,768]{1,0:T(8,128)(2,1)}), bf16[288,768]{1,0:T(8,128)(2,1)}) %reduce-scatter.11.cloned.1.call-update) | async-done | bytes 442384 | tf_op jit(solution)/shard_map/reduce_scatter | solution.py:227
  410.7 67.9 %reduce-scatter.9.cloned.1.call-done = bf16[192,2304]{1,0:T(8,128)(2,1)} async-done(((bf16[768,2304]{1,0:T(8,128)(2,1)}), bf16[192,2304]{1,0:T(8,128)(2,1)}) %reduce-scatter.9.cloned.1.call-update) | async-done | bytes 884752 | tf_op jit(solution)/shard_map/reduce_scatter | solution.py:224
  478.6 69.0 %reduce-scatter.5.cloned.1.call-done = bf16[192,2304]{1,0:T(8,128)(2,1)} async-done(((bf16[768,2304]{1,0:T(8,128)(2,1)}), bf16[192,2304]{1,0:T(8,128)(2,1)}) %reduce-scatter.5.cloned.1.call-update) | async-done | bytes 884752 | tf_op jit(solution)/shard_map/reduce_scatter | solution.py:218
  548.7 3.5 fusion.47
  552.6 10.7 %all-reduce.6 = (bf16[768]{0:T(1024)(128)(2,1)S(1)}, bf16[768]{0:T(1024)(128)(2,1)S(1)}) all-reduce(bf16[768]{0:T(1024)(128)(2,1)S(1)} %get-tuple-element.10, bf16[768]{0:T(1024)(128)(2,1)S(1)} %copy-done.43), channel_id=7, replica_groups=mesh['dp'=4,'ctx'=8] {'dp'}, use_global_device_ids=true, to_apply=%region_20.21.clone | all-reduce | flops 1536 | bytes 6144
  563.5 12.1 %all-reduce.4 = (bf16[192]{0:T(256)(128)(2,1)S(1)}, bf16[192]{0:T(256)(128)(2,1)S(1)}) all-reduce(bf16[192]{0:T(256)(128)(2,1)S(1)} %dynamic-slice.3, bf16[192]{0:T(256)(128)(2,1)S(1)} %dynamic-slice.5), channel_id=1, replica_groups=mesh['dp'=4,'ctx'=8] {'ctx'}, use_global_device_ids=true, to_apply=%region_21.22 | all-reduce | flops 384 | bytes 1536 | tf_op jit(solution)/shard_map/psum | solution.py:242
  577.7 39.2 %all-reduce.10.cloned.1.call-done = (bf16[192,2304]{1,0:T(8,128)(2,1)}, bf16[192,768]{1,0:T(8,128)(2,1)}, bf16[192,2304]{1,0:T(8,128)(2,1)}, bf16[288,768]{1,0:T(8,128)(2,1)}) async-done(((bf16[192,2304]{1,0:T(8,128)(2,1)}, bf16[192,768]{1,0:T(8,128)(2,1)}, bf16[192,2304]{1,0:T(8,128)(2,1)}, bf16[288,768]{1,0:T(8,128)(2,1)}), (bf16[192,2304]{1,0:T(8,128)(2,1)}, bf16[192,768]{1,0:T(8,128)(2,1)}, ...) | async-done | bytes 2506768 | tf_op jit(solution)/shard_map/psum | solution.py:238
  616.9 2.6 convert_element_type.150
  619.5 1.8 convert_element_type.152
  621.3 1.3 convert_element_type.154
  (178 shorter events, 22.5 us)
Async XLA Ops:
  7.2 75.2 %all-gather.10.cloned.1.call-start = ((), (), s32[]{:S(2)}) async-start(), calls=%async_computation.4 | async-start | bytes 4423680 | tf_op jit(solution)/shard_map/all_gather | solution.py:66
  7.9 106.1 %all-gather.14.cloned.1.call-start = ((), (), s32[]{:S(2)}) async-start(), calls=%async_computation.6 | async-start | bytes 1769472 | tf_op jit(solution)/shard_map/all_gather | solution.py:90
  26.1 89.7 %copy-start.22 = (f32[128,64]{0,1:T(8,128)}, f32[128,64]{0,1:T(8,128)S(1)}, u32[]{:S(2)}) copy-start(f32[128,64]{0,1:T(8,128)S(1)} %get-tuple-element.49) | copy-start | bytes 98308
  27.3 57.9 %copy-start.34 = (f32[128]{0:T(128)}, f32[128]{0:T(128)S(1)}, u32[]{:S(2)}) copy-start(f32[128]{0:T(128)S(1)} %broadcast_multiply_fusion.6) | copy-start | bytes 1540
  28.4 56.8 %copy-start.47 = (f32[128]{0:T(128)}, f32[128]{0:T(128)S(1)}, u32[]{:S(2)}) copy-start(f32[128]{0:T(128)S(1)} %fusion.46) | copy-start | bytes 1540
  28.5 56.8 %copy-start.36 = (f32[128]{0:T(128)}, f32[128]{0:T(128)S(1)}, u32[]{:S(2)}) copy-start(f32[128]{0:T(128)S(1)} %fusion.62) | copy-start | bytes 1540
  85.4 4.1 copy-start.4
  85.7 6.4 %copy-start.6 = (f32[128,12,64]{0,2,1:T(8,128)}, f32[128,12,64]{0,2,1:T(8,128)S(1)}, u32[]{:S(2)}) copy-start(f32[128,12,64]{0,2,1:T(8,128)S(1)} %get-tuple-element.45) | copy-start | bytes 1179652
  85.7 6.4 %copy-start.44 = (s32[1,128]{1,0:T(1,128)S(1)}, s32[1,128]{1,0:T(1,128)}, u32[]{:S(2)}) copy-start(s32[1,128]{1,0:T(1,128)} %param.10) | copy-start | bytes 1540
  89.6 52.1 %all-gather.12.cloned.1.call-start = ((), (), s32[]{:S(2)}) async-start(), calls=%async_computation.5 | async-start | bytes 1769472 | tf_op jit(solution)/shard_map/all_gather | solution.py:91
  90.4 83.2 %all-gather.16.cloned.1.call-start = ((), (), s32[]{:S(2)}) async-start(), calls=%async_computation.7 | async-start | bytes 1474560 | tf_op jit(solution)/shard_map/all_gather | solution.py:67
  90.9 153.2 %all-gather.18.cloned.1.call-start = ((), (), s32[]{:S(2)}) async-start(), calls=%async_computation.8 | async-start | bytes 4423680 | tf_op jit(solution)/shard_map/all_gather | solution.py:68
  91.5 192.9 %all-gather.20.cloned.1.call-start = ((), (), s32[]{:S(2)}) async-start(), calls=%async_computation.9 | async-start | bytes 2211840 | tf_op jit(solution)/shard_map/all_gather | solution.py:69
  92.1 219.4 %all-gather.22.cloned.1.call-start = ((), (), s32[]{:S(2)}) async-start(), calls=%async_computation.10 | async-start | bytes 1769472 | tf_op jit(solution)/shard_map/all_gather | solution.py:178
  100.9 16.1 %copy-start.31 = (s32[1,1024]{1,0:T(1,128)}, s32[1,1024]{1,0:T(1,128)S(1)}, u32[]{:S(2)}) copy-start(s32[1,1024]{1,0:T(1,128)S(1)} %all-gather) | copy-start | bytes 12292
  101.0 43.2 %copy-start.17 = (pred[128,1024]{1,0:T(8,128)(4,1)}, pred[128,1024]{1,0:T(8,128)(4,1)S(1)}, u32[]{:S(2)}) copy-start(pred[128,1024]{1,0:T(8,128)(4,1)S(1)} %broadcast_compare_fusion.1) | copy-start | bytes 393220
  101.1 239.2 %all-gather.24.cloned.1.call-start = ((), (), s32[]{:S(2)}) async-start(), calls=%async_computation.11 | async-start | bytes 1769472 | tf_op jit(solution)/shard_map/all_gather | solution.py:179
  121.7 28.3 %copy-start.32 = (f32[12,128]{1,0:T(8,128)}, f32[12,128]{1,0:T(8,128)S(1)}, u32[]{:S(2)}) copy-start(f32[12,128]{1,0:T(8,128)S(1)} %fusion.1) | copy-start | bytes 18436
  144.2 29.3 %copy-start.2 = (bf16[1,128,768]{2,1,0:T(8,128)(2,1)S(1)}, bf16[1,128,768]{2,1,0:T(8,128)(2,1)}, u32[]{:S(2)}) copy-start(bf16[1,128,768]{2,1,0:T(8,128)(2,1)} %param.9) | copy-start | bytes 589828
  150.0 26.0 %copy-start.21 = (bf16[128,12,64]{0,2,1:T(8,128)(2,1)}, bf16[128,12,64]{0,2,1:T(8,128)(2,1)S(1)}, u32[]{:S(2)}) copy-start(bf16[128,12,64]{0,2,1:T(8,128)(2,1)S(1)} %get-tuple-element.54) | copy-start | bytes 589828
  175.2 109.2 %copy-start.14 = (bf16[1,128,768]{2,1,0:T(8,128)(2,1)S(1)}, bf16[1,128,768]{2,1,0:T(8,128)(2,1)}, u32[]{:S(2)}) copy-start(bf16[1,128,768]{2,1,0:T(8,128)(2,1)} %param.17) | copy-start | bytes 589828
  284.5 4.2 copy-start.1
  284.5 4.2 copy-start.39
  284.5 4.2 copy-start.41
  287.8 2.8 copy-start.19
  290.6 4.4 copy-start.10
  292.3 4.7 copy-start.9
  292.3 79.2 %reduce-scatter.7.cloned.1.call-start = ((), (), s32[]{:S(2)}) async-start(), calls=%async_computation.13 | async-start | bytes 1474560 | tf_op jit(solution)/shard_map/reduce_scatter | solution.py:221
  294.9 115.8 %reduce-scatter.11.cloned.1.call-start = ((), (), s32[]{:S(2)}) async-start(), calls=%async_computation.15 | async-start | bytes 2211840 | tf_op jit(solution)/shard_map/reduce_scatter | solution.py:227
  296.9 5.7 copy-start.12
  296.9 181.7 %reduce-scatter.9.cloned.1.call-start = ((), (), s32[]{:S(2)}) async-start(), calls=%async_computation.14 | async-start | bytes 4423680 | tf_op jit(solution)/shard_map/reduce_scatter | solution.py:224
  300.9 34.1 %copy-start.5 = (f32[128,768]{0,1:T(8,128)S(1)}, f32[128,768]{0,1:T(8,128)}, u32[]{:S(2)}) copy-start(f32[128,768]{0,1:T(8,128)} %copy-done.4) | copy-start | bytes 1179652
  300.9 34.1 %copy-start.7 = (f32[128,12,64]{0,2,1:T(8,128)S(1)}, f32[128,12,64]{0,2,1:T(8,128)}, u32[]{:S(2)}) copy-start(f32[128,12,64]{0,2,1:T(8,128)} %copy-done.6) | copy-start | bytes 1179652
  300.9 246.6 %reduce-scatter.5.cloned.1.call-start = ((), (), s32[]{:S(2)}) async-start(), calls=%async_computation.12 | async-start | bytes 4423680 | tf_op jit(solution)/shard_map/reduce_scatter | solution.py:218
  314.8 10.1 %copy-start.33 = (f32[12,128]{1,0:T(8,128)}, f32[12,128]{1,0:T(8,128)S(1)}, u32[]{:S(2)}) copy-start(f32[12,128]{1,0:T(8,128)S(1)} %log_add_fusion) | copy-start | bytes 18436
  340.2 2.7 copy-start.30
  343.0 9.0 %copy-start.18 = (pred[128,1024]{1,0:T(8,128)(4,1)S(1)}, pred[128,1024]{1,0:T(8,128)(4,1)}, u32[]{:S(2)}) copy-start(pred[128,1024]{1,0:T(8,128)(4,1)} %copy-done.17) | copy-start | bytes 393220
  361.6 5.7 copy-start.35
  361.6 5.7 copy-start.37
  370.3 177.3 %copy-start.11 = (bf16[128,1152]{1,0:T(8,128)(2,1)S(1)}, bf16[128,1152]{1,0:T(8,128)(2,1)}, u32[]{:S(2)}) copy-start(bf16[128,1152]{1,0:T(8,128)(2,1)} %get-tuple-element.27) | copy-start | bytes 884740
  370.3 177.3 %copy-start.13 = (bf16[1152,768]{1,0:T(8,128)(2,1)S(1)}, bf16[1152,768]{1,0:T(8,128)(2,1)}, u32[]{:S(2)}) copy-start(bf16[1152,768]{1,0:T(8,128)(2,1)} %all-gather.20.cloned.1.call-done) | copy-start | bytes 5308420
  370.3 246.5 %all-reduce.10.cloned.1.call-start = ((), (), s32[]{:S(2)}) async-start(), calls=%async_computation.16 | async-start | bytes 5013504 | tf_op jit(solution)/shard_map/psum | solution.py:238
  548.7 3.5 copy-start.48
  548.7 3.8 copy-start.43
  548.7 28.0 %copy-start.15 = (bf16[1,128,768]{2,1,0:T(8,128)(2,1)S(1)}, bf16[1,128,768]{2,1,0:T(8,128)(2,1)}, u32[]{:S(2)}) copy-start(bf16[1,128,768]{2,1,0:T(8,128)(2,1)} %param.17) | copy-start | bytes 589828
  548.7 28.0 %copy-start.46 = (f32[128]{0:T(128)S(1)}, f32[128]{0:T(128)}, u32[]{:S(2)}) copy-start(f32[128]{0:T(128)} %copy-done.45) | copy-start | bytes 1540
  616.9 4.4 copy-start.20
  616.9 5.7 copy-start.23
  (16 other events, 32.4 us)
Sparse Core Ops, SparseCore 0:
  9.6 72.7 all-gather.9
  89.7 24.2 all-gather.13
  115.9 25.6 all-gather.11
  143.0 30.4 all-gather.15
  174.9 69.0 all-gather.17
  245.5 38.8 all-gather.19
  286.9 24.5 all-gather.21
  313.4 25.8 all-gather.23
  341.6 29.1 reduce-scatter.6
  373.6 37.0 reduce-scatter.10
  413.1 65.4 reduce-scatter.8
  480.9 66.6 reduce-scatter.4
  551.7 65.0 all-reduce.9
where the time goes:
time: 631 us; the launch traced here: 630 us
  waiting for transfers between devices  441 us (70%)
  blocking collectives  64.3 us (10%)
  matrix products  62.8 us (10%)
  other arithmetic  24.1 us (4%)
  local copies, waits for them, and re-layouts  21.3 us (3%)
  between operations  16 us (3%)
    reduce_scatter x1, waiting for transfers between devices, local(): lax.psum_scatter(local_grads[0].astype(jnp.bfloat16), 'dp', scatter_dimen...  69 us
    all_gather x1, waiting for transfers between devices, local(): lax.all_gather(shards[2], 'dp', axis=0, tiled=True)  68.1 us
    reduce_scatter x1, waiting for transfers between devices, local(): lax.psum_scatter(local_grads[2].astype(jnp.bfloat16), 'dp', scatter_dimen...  67.9 us
    all_gather x1, waiting for transfers between devices, local(): lax.all_gather(shards[0], 'dp', axis=0, tiled=True)  53.9 us
    reduce_scatter x1, waiting for transfers between devices, local(): lax.psum_scatter(local_grads[3].astype(jnp.bfloat16), 'dp', scatter_dimen...  39.2 us
    psum x1, waiting for transfers between devices, local(): lax.psum(shares[0].astype(jnp.bfloat16), 'ctx').astype(jnp.float32)  39.2 us
    all_gather x1, waiting for transfers between devices, local(): lax.all_gather(shards[3], 'dp', axis=0, tiled=True)  37.7 us
    unnamed x2, blocking collectives  24.3 us
  transfers between devices with their start and end apart: 13, of which 11 were waited for; matrix products, arithmetic and copies ran while one was open for 14% of the time, Pallas kernels for 0%

commit v1 on v0

--- a/solution.py
+++ b/solution.py
@@ -88,7 +88,12 @@
     query_flat = queries.reshape(local_rows, model_width)
     highest = jnp.full((head_count, local_rows), NEGATIVE, jnp.float32)
     block_keys = lax.all_gather(key_flat, "ctx", axis=0, tiled=True)
-    block_values = lax.all_gather(value_flat, "ctx", axis=0, tiled=True)
+    ring = [value_flat]
+    for hop in range(7):
+        ring.append(lax.ppermute(ring[-1], "ctx", [(dev, (dev + 1) % 8) for dev in range(8)]))
+    block_values = jnp.roll(
+        jnp.concatenate(ring[::-1], axis=0), (lax.axis_index("ctx") + 1) * ring[0].shape[0], axis=0
+    )
     block_ids = lax.all_gather(own_ids, "ctx", axis=0, tiled=True)
     piece_rows = block_keys.shape[0]
     scores = (

time: 631 us -> 634 us (level)
    ppermute x0 -> x7, waiting for transfers between devices: none -> 35.8 us  [local(): lax.ppermute(ring[-1], 'ctx', [(dev, (dev + 1) % 8) for dev in range(8)])]
    all_gather x1, waiting for transfers between devices: 23.5 us -> 0.01 us  [local(): lax.all_gather(shards[1], 'dp', axis=0, tiled=True)]
    all_gather x1, waiting for transfers between devices: 12.9 us -> 0.01 us  [local(): block_keys = lax.all_gather(key_flat, 'ctx', axis=0, tiled=True)]
  transfers between devices with their start and end apart: 13 -> 20, of which waited for: 11 -> 15; matrix products, arithmetic and copies ran while one was open for 14% -> 14% of each run, Pallas kernels for 0% -> 0%
where the time goes in v1:
time: 634 us; the launch traced here: 633 us
  waiting for transfers between devices  443 us (70%)
  blocking collectives  66.8 us (11%)
  matrix products  59.7 us (9%)
  other arithmetic  23.3 us (4%)
  local copies, waits for them, and re-layouts  22.1 us (3%)
  between operations  16.2 us (3%)
    reduce_scatter x1, waiting for transfers between devices, local(): lax.psum_scatter(local_grads[0].astype(jnp.bfloat16), 'dp', scatter_dimen...  69 us
    reduce_scatter x1, waiting for transfers between devices, local(): lax.psum_scatter(local_grads[2].astype(jnp.bfloat16), 'dp', scatter_dimen...  67.9 us
    all_gather x1, waiting for transfers between devices, local(): lax.all_gather(shards[2], 'dp', axis=0, tiled=True)  64.9 us
    all_gather x1, waiting for transfers between devices, local(): lax.all_gather(shards[0], 'dp', axis=0, tiled=True)  53.3 us
    psum x1, waiting for transfers between devices, local(): lax.psum(shares[0].astype(jnp.bfloat16), 'ctx').astype(jnp.float32)  39.2 us
    reduce_scatter x1, waiting for transfers between devices, local(): lax.psum_scatter(local_grads[3].astype(jnp.bfloat16), 'dp', scatter_dimen...  38.9 us
    all_gather x1, waiting for transfers between devices, local(): lax.all_gather(shards[3], 'dp', axis=0, tiled=True)  37.7 us
    ppermute x7, waiting for transfers between devices, local(): lax.ppermute(ring[-1], 'ctx', [(dev, (dev + 1) % 8) for dev in range(8)])  35.8 us
  transfers between devices with their start and end apart: 20, of which 15 were waited for; matrix products, arithmetic and copies ran while one was open for 14% of the time, Pallas kernels for 0%

profile of v1, /device:TPU:0, one launch (start us, length us, event | category | flops | bytes accessed | tf_op | source)
XLA Modules:
  0.0 632.6 jit_solution(15776542721608258040)
XLA Ops:
  8.0 1.3 fusion.87
  11.6 13.6 %all-reduce.7 = (bf16[768]{0:T(1024)(128)(2,1)S(1)}, bf16[768]{0:T(1024)(128)(2,1)S(1)}) all-reduce(bf16[768]{0:T(1024)(128)(2,1)S(1)} %dynamic-update-slice, bf16[768]{0:T(1024)(128)(2,1)S(1)} %dynamic-update-slice.1), channel_id=1, replica_groups=mesh['dp'=4,'ctx'=8] {'dp'}, use_global_device_ids=true, to_apply=%add | all-reduce | flops 1536 | bytes 6144
  29.0 53.3 %all-gather.10.cloned.1.call-done = bf16[768,2304]{1,0:T(8,128)(2,1)} async-done(((bf16[192,2304]{1,0:T(8,128)(2,1)}), bf16[768,2304]{1,0:T(8,128)(2,1)}) %all-gather.10.cloned.1.call-update) | async-done | bytes 3538960 | tf_op jit(solution)/shard_map/all_gather | solution.py:66
  82.3 2.8 fusion.78
  87.6 2.0 add_convert_fusion.2
  92.2 6.0 collective-permute-done
  98.2 6.0 collective-permute-done.1
  104.2 6.1 collective-permute-done.2
  110.3 6.2 collective-permute-done.3
  116.5 6.0 collective-permute-done.4
  122.5 10.9 %all-gather = s32[1,1024]{1,0:T(1,128)S(1)} all-gather(s32[1,128]{1,0:T(1,128)S(1)} %copy-done.49), channel_id=2, replica_groups=mesh['dp'=4,'ctx'=8] {'ctx'}, dimensions={1}, use_global_device_ids=true | all-gather | bytes 4608 | tf_op jit(solution)/shard_map/all_gather | solution.py:97
  134.0 5.5 collective-permute-done.6
  141.9 1.6 copy.45
  143.5 1.7 copy.50
  145.3 1.3 select_reduce_fusion
  146.6 1.9 fusion.1
  149.2 2.5 fusion.88
  151.8 1.8 fusion.89
  154.3 64.9 %all-gather.16.cloned.1.call-done = bf16[768,2304]{1,0:T(8,128)(2,1)} async-done(((bf16[192,2304]{1,0:T(8,128)(2,1)}), bf16[768,2304]{1,0:T(8,128)(2,1)}) %all-gather.16.cloned.1.call-update) | async-done | bytes 3538960 | tf_op jit(solution)/shard_map/all_gather | solution.py:68
  219.2 2.7 fusion.81
  221.9 37.7 %all-gather.18.cloned.1.call-done = bf16[1152,768]{1,0:T(8,128)(2,1)} async-done(((bf16[288,768]{1,0:T(8,128)(2,1)}), bf16[1152,768]{1,0:T(8,128)(2,1)}) %all-gather.18.cloned.1.call-update) | async-done | bytes 1769488 | tf_op jit(solution)/shard_map/all_gather | solution.py:69
  259.5 3.3 add_convert_fusion
  263.8 1.9 multiply_reduce_fusion
  267.3 2.5 convolution_convert_fusion.3
  269.9 1.9 convolution_convert_fusion.2
  271.9 4.0 convolution_convert_fusion
  278.0 8.4 %all-gather.22.cloned.1.call-done = bf16[1024,768]{1,0:T(8,128)(2,1)} async-done(((bf16[128,768]{1,0:T(8,128)(2,1)}), bf16[1024,768]{1,0:T(8,128)(2,1)}) %all-gather.22.cloned.1.call-update) | async-done | bytes 1572880 | tf_op jit(solution)/shard_map/all_gather | solution.py:183
  286.4 2.6 copy.55
  289.0 25.0 %all-gather.20.cloned.1.call-done = bf16[1024,768]{1,0:T(8,128)(2,1)} async-done(((bf16[128,768]{1,0:T(8,128)(2,1)}), bf16[1024,768]{1,0:T(8,128)(2,1)}) %all-gather.20.cloned.1.call-update) | async-done | bytes 1572880 | tf_op jit(solution)/shard_map/all_gather | solution.py:163
  314.1 2.6 copy.52
  317.4 10.1 %all_gather.58 = f32[12,1024]{1,0:T(8,128)} all-gather(f32[12,128]{1,0:T(8,128)S(1)} %log_add_fusion), channel_id=1, replica_groups=mesh['dp'=4,'ctx'=8] {'ctx'}, dimensions={1}, use_global_device_ids=true | all-gather | bytes 55296 | tf_op jit(solution)/shard_map/all_gather | solution.py:158
  328.5 9.4 %all_gather.60 = f32[12,1024]{1,0:T(8,128)} all-gather(f32[12,128]{1,0:T(8,128)S(1)} %bitcast.132), channel_id=1, replica_groups=mesh['dp'=4,'ctx'=8] {'ctx'}, dimensions={1}, use_global_device_ids=true | all-gather | bytes 55296 | tf_op jit(solution)/shard_map/all_gather | solution.py:159
  337.9 5.2 fusion.54
  343.1 2.6 copy.56
  345.8 9.0 %fusion.17 = f32[128,12,64]{0,2,1:T(8,128)} fusion(bf16[1024,12,64]{0,2,1:T(8,128)(2,1)} %bitcast.106, f32[12,1024,128]{2,1,0:T(8,128)} %fusion.54, f32[12,1024]{1,0:T(8,128)S(1)} %copy-done.34, f32[12,1024]{1,0:T(8,128)S(1)} %copy-done.32, pred[1024,128]{1,0:T(8,128)(4,1)S(1)} %copy-done.30, bf16[1024,12,64]{0,2,1:T(8,128)(2,1)} %bitcast.113, ...), kind=kOutput, calls=%fused_computation.22 | convolution fusion | flops 412090368 | bytes 10256384 | tf_op jit(solution)/shard_map/hqk,qhe->khe/dot_general | solution.py:204
  354.8 7.1 %broadcast_multiply_fusion.1 = (f32[128,12,64]{0,2,1:T(8,128)}, f32[128,12,64]{0,2,1:T(8,128)S(1)}, f32[128,12,64]{0,2,1:T(8,128)}) fusion(f32[128,64]{0,1:T(8,128)} %get-tuple-element.47, f32[128,12,64]{0,2,1:T(8,128)} %fusion.17, bf16[1024,12,64]{0,2,1:T(8,128)(2,1)S(1)} %bitcast.104, f32[12,128,1024]{2,1,0:T(8,128)} %copy-done, ...), kind=kOutput, calls=%fused_computation.102 | convolution fusion | flops 412286976 | bytes 11382784 | tf_op jit(solution)/shard_map/hqk,khe->qhe/dot_general | solution.py:180
  364.4 5.0 fusion.23
  370.1 3.0 convolution_convert_fusion.1
  374.3 38.9 %reduce-scatter.11.cloned.1.call-done = bf16[288,768]{1,0:T(8,128)(2,1)} async-done(((bf16[1152,768]{1,0:T(8,128)(2,1)}), bf16[288,768]{1,0:T(8,128)(2,1)}) %reduce-scatter.11.cloned.1.call-update) | async-done | bytes 442384 | tf_op jit(solution)/shard_map/reduce_scatter | solution.py:232
  413.2 67.9 %reduce-scatter.9.cloned.1.call-done = bf16[192,2304]{1,0:T(8,128)(2,1)} async-done(((bf16[768,2304]{1,0:T(8,128)(2,1)}), bf16[192,2304]{1,0:T(8,128)(2,1)}) %reduce-scatter.9.cloned.1.call-update) | async-done | bytes 884752 | tf_op jit(solution)/shard_map/reduce_scatter | solution.py:229
  481.2 69.0 %reduce-scatter.5.cloned.1.call-done = bf16[192,2304]{1,0:T(8,128)(2,1)} async-done(((bf16[768,2304]{1,0:T(8,128)(2,1)}), bf16[192,2304]{1,0:T(8,128)(2,1)}) %reduce-scatter.5.cloned.1.call-update) | async-done | bytes 884752 | tf_op jit(solution)/shard_map/reduce_scatter | solution.py:223
  551.3 3.5 fusion.47
  555.1 10.8 %all-reduce.6 = (bf16[768]{0:T(1024)(128)(2,1)S(1)}, bf16[768]{0:T(1024)(128)(2,1)S(1)}) all-reduce(bf16[768]{0:T(1024)(128)(2,1)S(1)} %get-tuple-element.10, bf16[768]{0:T(1024)(128)(2,1)S(1)} %copy-done.48), channel_id=7, replica_groups=mesh['dp'=4,'ctx'=8] {'dp'}, use_global_device_ids=true, to_apply=%region_20.21.clone | all-reduce | flops 1536 | bytes 6144
  566.0 12.1 %all-reduce.4 = (bf16[192]{0:T(256)(128)(2,1)S(1)}, bf16[192]{0:T(256)(128)(2,1)S(1)}) all-reduce(bf16[192]{0:T(256)(128)(2,1)S(1)} %dynamic-slice.3, bf16[192]{0:T(256)(128)(2,1)S(1)} %dynamic-slice.5), channel_id=1, replica_groups=mesh['dp'=4,'ctx'=8] {'ctx'}, use_global_device_ids=true, to_apply=%region_21.22 | all-reduce | flops 384 | bytes 1536 | tf_op jit(solution)/shard_map/psum | solution.py:247
  580.2 39.2 %all-reduce.10.cloned.1.call-done = (bf16[192,2304]{1,0:T(8,128)(2,1)}, bf16[192,768]{1,0:T(8,128)(2,1)}, bf16[192,2304]{1,0:T(8,128)(2,1)}, bf16[288,768]{1,0:T(8,128)(2,1)}) async-done(((bf16[192,2304]{1,0:T(8,128)(2,1)}, bf16[192,768]{1,0:T(8,128)(2,1)}, bf16[192,2304]{1,0:T(8,128)(2,1)}, bf16[288,768]{1,0:T(8,128)(2,1)}), (bf16[192,2304]{1,0:T(8,128)(2,1)}, bf16[192,768]{1,0:T(8,128)(2,1)}, ...) | async-done | bytes 2506768 | tf_op jit(solution)/shard_map/psum | solution.py:243
  619.4 2.6 convert_element_type.150
  622.0 1.8 convert_element_type.152
  623.8 1.3 convert_element_type.154
  (222 shorter events, 30.1 us)
Async XLA Ops:
  7.2 75.2 %all-gather.10.cloned.1.call-start = ((), (), s32[]{:S(2)}) async-start(), calls=%async_computation.4 | async-start | bytes 4423680 | tf_op jit(solution)/shard_map/all_gather | solution.py:66
  7.9 135.6 %all-gather.12.cloned.1.call-start = ((), (), s32[]{:S(2)}) async-start(), calls=%async_computation.5 | async-start | bytes 1769472 | tf_op jit(solution)/shard_map/all_gather | solution.py:90
  27.9 57.3 %copy-start.39 = (f32[128]{0:T(128)}, f32[128]{0:T(128)S(1)}, u32[]{:S(2)}) copy-start(f32[128]{0:T(128)S(1)} %broadcast_multiply_fusion.6) | copy-start | bytes 1540
  29.0 56.2 %copy-start.53 = (f32[128]{0:T(128)}, f32[128]{0:T(128)S(1)}, u32[]{:S(2)}) copy-start(f32[128]{0:T(128)S(1)} %fusion.46) | copy-start | bytes 1540
  29.0 56.2 %copy-start.41 = (f32[128]{0:T(128)}, f32[128]{0:T(128)S(1)}, u32[]{:S(2)}) copy-start(f32[128]{0:T(128)S(1)} %fusion.62) | copy-start | bytes 1540
  85.7 6.4 %copy-start.6 = (f32[128,12,64]{0,2,1:T(8,128)}, f32[128,12,64]{0,2,1:T(8,128)S(1)}, u32[]{:S(2)}) copy-start(f32[128,12,64]{0,2,1:T(8,128)S(1)} %get-tuple-element.45) | copy-start | bytes 1179652
  85.7 36.8 %copy-start.49 = (s32[1,128]{1,0:T(1,128)S(1)}, s32[1,128]{1,0:T(1,128)}, u32[]{:S(2)}) copy-start(s32[1,128]{1,0:T(1,128)} %param.10) | copy-start | bytes 1540
  89.6 62.2 %all-gather.14.cloned.1.call-start = ((), (), s32[]{:S(2)}) async-start(), calls=%async_computation.6 | async-start | bytes 1474560 | tf_op jit(solution)/shard_map/all_gather | solution.py:67
  90.3 128.9 %all-gather.16.cloned.1.call-start = ((), (), s32[]{:S(2)}) async-start(), calls=%async_computation.7 | async-start | bytes 4423680 | tf_op jit(solution)/shard_map/all_gather | solution.py:68
  90.9 168.6 %all-gather.18.cloned.1.call-start = ((), (), s32[]{:S(2)}) async-start(), calls=%async_computation.8 | async-start | bytes 2211840 | tf_op jit(solution)/shard_map/all_gather | solution.py:69
  91.5 195.0 %all-gather.22.cloned.1.call-start = ((), (), s32[]{:S(2)}) async-start(), calls=%async_computation.10 | async-start | bytes 1769472 | tf_op jit(solution)/shard_map/all_gather | solution.py:183
  92.1 222.0 %all-gather.20.cloned.1.call-start = ((), (), s32[]{:S(2)}) async-start(), calls=%async_computation.9 | async-start | bytes 1769472 | tf_op jit(solution)/shard_map/all_gather | solution.py:163
  92.1 41.6 %copy-start.12 = (bf16[128,768]{1,0:T(8,128)(2,1)}, bf16[128,768]{1,0:T(8,128)(2,1)S(1)}, u32[]{:S(2)}) copy-start(bf16[128,768]{1,0:T(8,128)(2,1)S(1)} %slice.89) | copy-start | bytes 589828
  92.2 6.0 collective-permute-start
  98.2 6.0 collective-permute-start.1
  104.2 6.1 collective-permute-start.2
  110.3 6.2 collective-permute-start.3
  116.5 6.0 collective-permute-start.4
  122.5 10.9 %collective-permute-start.5 = (bf16[128,768]{1,0:T(8,128)(2,1)S(1)}, bf16[128,768]{1,0:T(8,128)(2,1)S(1)}, u32[]{:S(2)}, u32[]{:S(2)}) collective-permute-start(bf16[128,768]{1,0:T(8,128)(2,1)S(1)} %collective-permute-done.4), channel_id=1, source_target_pairs={{0,1},{1,2},{2,3},{3,4},{4,5},{5,6},{6,7},{7,0},{8,9},{9,10},{10,1... | collective-permute-start | bytes 589832 | tf_op jit(solution)/shard_map/ppermute | solution.py:93
  133.4 8.4 %copy-start.35 = (s32[1,1024]{1,0:T(1,128)}, s32[1,1024]{1,0:T(1,128)S(1)}, u32[]{:S(2)}) copy-start(s32[1,1024]{1,0:T(1,128)S(1)} %all-gather) | copy-start | bytes 12292
  133.4 6.1 collective-permute-start.6
  133.8 14.8 %copy-start.20 = (pred[128,1024]{1,0:T(8,128)(4,1)}, pred[128,1024]{1,0:T(8,128)(4,1)S(1)}, u32[]{:S(2)}) copy-start(pred[128,1024]{1,0:T(8,128)(4,1)S(1)} %broadcast_compare_fusion.1) | copy-start | bytes 393220
  133.8 209.3 %all-gather.24.cloned.1.call-start = ((), (), s32[]{:S(2)}) async-start(), calls=%async_computation.11 | async-start | bytes 1769472 | tf_op jit(solution)/shard_map/all_gather | solution.py:184
  153.6 106.0 %copy-start.16 = (bf16[1,128,768]{2,1,0:T(8,128)(2,1)S(1)}, bf16[1,128,768]{2,1,0:T(8,128)(2,1)}, u32[]{:S(2)}) copy-start(bf16[1,128,768]{2,1,0:T(8,128)(2,1)} %param.17) | copy-start | bytes 589828
  259.5 4.2 copy-start.44
  259.5 4.2 copy-start.46
  265.6 4.3 copy-start.10
  267.3 4.6 copy-start.9
  267.3 107.0 %reduce-scatter.7.cloned.1.call-start = ((), (), s32[]{:S(2)}) async-start(), calls=%async_computation.13 | async-start | bytes 1474560 | tf_op jit(solution)/shard_map/reduce_scatter | solution.py:226
  269.8 143.4 %reduce-scatter.11.cloned.1.call-start = ((), (), s32[]{:S(2)}) async-start(), calls=%async_computation.15 | async-start | bytes 2211840 | tf_op jit(solution)/shard_map/reduce_scatter | solution.py:232
  271.8 4.4 copy-start.36
  271.8 4.4 copy-start.50
  271.8 5.2 copy-start.13
  271.8 209.3 %reduce-scatter.9.cloned.1.call-start = ((), (), s32[]{:S(2)}) async-start(), calls=%async_computation.14 | async-start | bytes 4423680 | tf_op jit(solution)/shard_map/reduce_scatter | solution.py:229
  275.9 274.2 %reduce-scatter.5.cloned.1.call-start = ((), (), s32[]{:S(2)}) async-start(), calls=%async_computation.12 | async-start | bytes 4423680 | tf_op jit(solution)/shard_map/reduce_scatter | solution.py:223
  278.0 59.9 %copy-start.5 = (f32[128,768]{0,1:T(8,128)S(1)}, f32[128,768]{0,1:T(8,128)}, u32[]{:S(2)}) copy-start(f32[128,768]{0,1:T(8,128)} %copy-done.4) | copy-start | bytes 1179652
  278.0 59.9 %copy-start.7 = (f32[128,12,64]{0,2,1:T(8,128)S(1)}, f32[128,12,64]{0,2,1:T(8,128)}, u32[]{:S(2)}) copy-start(f32[128,12,64]{0,2,1:T(8,128)} %copy-done.6) | copy-start | bytes 1179652
  317.4 10.1 %copy-start.38 = (f32[12,128]{1,0:T(8,128)}, f32[12,128]{1,0:T(8,128)S(1)}, u32[]{:S(2)}) copy-start(f32[12,128]{1,0:T(8,128)S(1)} %log_add_fusion) | copy-start | bytes 18436
  345.8 9.0 %copy-start.21 = (pred[128,1024]{1,0:T(8,128)(4,1)S(1)}, pred[128,1024]{1,0:T(8,128)(4,1)}, u32[]{:S(2)}) copy-start(pred[128,1024]{1,0:T(8,128)(4,1)} %copy-done.20) | copy-start | bytes 393220
  364.4 5.7 copy-start.40
  364.4 5.7 copy-start.42
  373.1 177.0 %copy-start.11 = (bf16[128,1152]{1,0:T(8,128)(2,1)S(1)}, bf16[128,1152]{1,0:T(8,128)(2,1)}, u32[]{:S(2)}) copy-start(bf16[128,1152]{1,0:T(8,128)(2,1)} %get-tuple-element.27) | copy-start | bytes 884740
  373.1 177.0 %copy-start.15 = (bf16[1152,768]{1,0:T(8,128)(2,1)S(1)}, bf16[1152,768]{1,0:T(8,128)(2,1)}, u32[]{:S(2)}) copy-start(bf16[1152,768]{1,0:T(8,128)(2,1)} %all-gather.18.cloned.1.call-done) | copy-start | bytes 5308420
  373.1 246.3 %all-reduce.10.cloned.1.call-start = ((), (), s32[]{:S(2)}) async-start(), calls=%async_computation.16 | async-start | bytes 5013504 | tf_op jit(solution)/shard_map/psum | solution.py:243
  551.3 28.0 %copy-start.17 = (bf16[1,128,768]{2,1,0:T(8,128)(2,1)S(1)}, bf16[1,128,768]{2,1,0:T(8,128)(2,1)}, u32[]{:S(2)}) copy-start(bf16[1,128,768]{2,1,0:T(8,128)(2,1)} %param.17) | copy-start | bytes 589828
  551.3 28.0 %copy-start.52 = (f32[128]{0:T(128)S(1)}, f32[128]{0:T(128)}, u32[]{:S(2)}) copy-start(f32[128]{0:T(128)} %copy-done.51) | copy-start | bytes 1540
  619.4 4.4 copy-start.23
  619.4 5.7 copy-start.27
  (29 other events, 70.3 us)
Sparse Core Ops, SparseCore 0:
  9.6 72.7 all-gather.9
  89.7 26.4 all-gather.11
  117.8 30.7 all-gather.13
  150.0 69.0 all-gather.15
  220.6 38.8 all-gather.17
  261.8 24.5 all-gather.21
  288.3 25.6 all-gather.19
  315.9 25.8 all-gather.23
  344.1 29.1 reduce-scatter.6
  376.1 37.0 reduce-scatter.10
  415.7 65.4 reduce-scatter.8
  483.4 66.6 reduce-scatter.4
  554.3 65.0 all-reduce.9
